TPU v7x, 128 devices: a whole 4x4x4 slice. The times are simulated.
128 devices in a mesh: grp: 4 (over z_lo, core), blk: 32 (over y, x, z_hi).
Axes of the slice: x: 4, y: 4, z: 4 (z_hi: 2, z_lo: 2; z = z_hi * 2 + z_lo), core: 2. Of those that a mesh axis runs over, the one named last changes fastest.
Arguments:
- embeddings: float32 [4, 4, 32, 128, 768], P(None, 'grp', 'blk')
- cluster_ids: int32 [4, 16384], P('grp'), may hold values from 0 to 63, as said below
Outputs:
- best_match: float32 [4, 16384], P('grp', 'blk')
Inputs may be any that keep to these rules, and one draw needn't show every extreme that they name: `cluster_ids`: along each group's row the ids never fall; group g holds clusters g * 16 to (g + 1) * 16 - 1, each with one point or more, and the largest of them has exactly 9216 points.
All inputs are finite; a program needn't handle non-finite values.
Results may differ from a plain program's by a relative error of at most 0.0003.
Values may be sent and summed in bfloat16 or wider, within the bound.
A program may use at most 128 MiB of HBM per device.

v0:
```python
import functools

import jax
import jax.numpy as jnp
from jax import lax
from jax.experimental import pallas as pl
from jax.experimental.pallas import tpu as pltpu
from jax.sharding import PartitionSpec as P

MESH = pl.DeviceIdType.MESH
D = 768
SLOTS = 5
PIECE = 32
STEPS = 16

SRC = [[0, 3, 0, 0], [3, 0, 0, 0], [0, 0, 4, 0], [0, 0, 4, 0], [0, 4, 1, 0], [4, 0, 2, 0], [0, 3, 0, 0], [3, 0, 0, 0],
       [3, 0, 0, 3], [0, 3, 0, 3], [2, 4, 0, 0], [4, 1, 0, 0], [2, 0, 4, 0], [0, 1, 4, 0], [4, 0, 0, 3], [0, 4, 0, 3]]
DEP = [[1, 1, 1, 2], [1, 1, 1, 2], [1, 2, 1, 1], [2, 1, 1, 1], [1, 2, 2, 1], [2, 1, 2, 1], [1, 2, 1, 2], [2, 1, 1, 2],
       [2, 2, 1, 2], [2, 2, 1, 2], [2, 1, 2, 1], [1, 2, 2, 1], [2, 1, 1, 1], [1, 2, 1, 1], [2, 1, 1, 1], [1, 2, 1, 1]]
BLK = [[1, 3, 4, 8], [2, 0, 5, 9], [3, 5, 6, 14], [4, 2, 7, 15], [5, 11, 12, 0], [10, 4, 13, 1], [7, 1, 10, 14],
       [0, 6, 11, 15], [13, 7, 12, 5], [6, 12, 13, 4], [8, 9, 2, 6], [8, 9, 3, 7], [14, 15, 0, 8], [14, 15, 1, 9],
       [11, 13, 2, 10], [12, 10, 3, 11]]
IDX = [[1, 1, 1, 1], [1, 1, 1, 1], [2, 2, 1, 1], [2, 2, 1, 1], [3, 1, 1, 2], [1, 3, 1, 2], [2, 3, 2, 2], [3, 2, 2, 2],
       [2, 3, 2, 4], [3, 3, 3, 4], [2, 2, 3, 4], [3, 3, 3, 4], [3, 3, 4, 4], [4, 4, 4, 4], [3, 4, 4, 3], [4, 4, 4, 4]]
HOLD = [[0, 1, 4, 7, 12], [1, 0, 5, 6, 13], [2, 1, 3, 10, 14], [3, 0, 2, 11, 15], [4, 0, 3, 5, 9], [5, 1, 2, 4, 8],
        [6, 2, 7, 9, 10], [7, 3, 6, 8, 11], [8, 0, 10, 11, 12], [9, 1, 10, 11, 13], [10, 5, 6, 14, 15], [11, 4, 7, 14, 15],
        [12, 4, 8, 9, 15], [13, 5, 8, 9, 14], [14, 2, 6, 12, 13], [15, 3, 7, 12, 13]]
PAIRS = [[[(1, 3), (1, 4), (3, 4)], [(0, 1), (0, 2), (1, 2)]], [[(2, 1), (2, 4), (1, 4)], [(0, 1), (0, 3), (3, 4)]],
         [[(1, 3), (3, 4), (2, 3), (2, 4)], [(0, 1), (0, 2), (1, 2)]],
         [[(2, 3), (2, 1), (1, 3)], [(0, 3), (3, 4), (0, 1)]], [[(4, 0), (4, 1), (0, 2), (1, 2)], [(0, 3), (1, 3)]],
         [[(2, 0), (4, 1), (2, 1)], [(0, 1), (0, 3), (1, 3)]], [[(1, 3), (1, 4), (3, 4)], [(0, 3), (2, 0), (2, 1)]],
         [[(2, 3), (2, 4), (3, 4)], [(2, 0), (1, 2), (1, 0)]],
         [[(2, 3), (2, 1), (0, 1), (3, 1)], [(4, 2), (4, 0), (2, 0)]],
         [[(4, 1), (4, 0), (4, 3), (1, 3)], [(1, 0), (1, 2), (0, 2)]],
         [[(3, 4), (3, 1), (4, 1)], [(2, 0), (1, 2), (1, 0)]], [[(1, 0), (3, 1), (3, 2)], [(4, 0), (4, 2), (2, 0)]],
         [[(3, 4), (4, 1), (0, 1)], [(4, 0), (4, 2), (0, 2)]], [[(3, 4), (4, 1), (1, 2)], [(4, 0), (4, 2), (0, 2)]],
         [[(3, 4), (3, 1), (4, 1)], [(2, 0), (1, 2), (1, 0)]], [[(3, 4), (3, 1), (4, 1)], [(3, 2), (2, 1), (2, 0)]]]
NEED = [[[1, 3, 4], [0, 1, 2]], [[1, 2, 4], [0, 1, 3, 4]], [[1, 2, 3, 4], [0, 1, 2]], [[1, 2, 3], [0, 1, 3, 4]],
        [[0, 1, 2, 4], [0, 1, 3]], [[0, 1, 2, 4], [0, 1, 3]], [[1, 3, 4], [0, 1, 2, 3]], [[2, 3, 4], [0, 1, 2]],
        [[0, 1, 2, 3], [0, 2, 4]], [[0, 1, 3, 4], [0, 1, 2]], [[1, 3, 4], [0, 1, 2]], [[0, 1, 2, 3], [0, 2, 4]],
        [[0, 1, 3, 4], [0, 2, 4]], [[1, 2, 3, 4], [0, 2, 4]], [[1, 3, 4], [0, 1, 2]], [[1, 3, 4], [0, 1, 2, 3]]]

REL = (0, 3, 1, 2)


def word(digits, base):
    total = 0
    for digit in reversed(digits):
        total = total * base + digit
    return total


def look_up(index, words):
    got = jnp.int32(words[0])
    for k in range(1, len(words)):
        got = jnp.where(index == k, jnp.int32(words[k]), got)
    return got


def digits_of(value, base, count):
    out = []
    for _ in range(count):
        out.append(value % base)
        value = value // base
    return out


def kernel(emb, ids_in, out, x, units, stage, ids_got, ids_rows, ids_cols, row_best, col_best, row_line, part, parts_got,
           relay,
           load_sem, id_send, id_recv, z_send, z_recv, relay_send, relay_recv, f_send, f_recv, c_send, c_recv, r_send, r_recv):
    grp, blk = lax.axis_index("grp"), lax.axis_index("blk")
    h, zl = grp % 2, grp // 2
    p, zh = blk // 2, blk % 2
    z = zh * 2 + zl
    px, py = p % 4, p // 4

    def device(z_of, core, chip):
        return ((z_of % 2) * 2 + core, chip * 2 + z_of // 2)

    def group_of(z_of):
        return (z_of % 2) * 2 + z_of // 2

    near = [py * 4 + (px + 1) % 4, py * 4 + (px + 3) % 4, ((py + 1) % 4) * 4 + px, ((py + 3) % 4) * 4 + px]
    first = look_up(p, [word(SRC[c], 8) + 4096 * word(DEP[c], 4) for c in range(16)])
    src = digits_of(first, 8, 4)
    dep = digits_of(first // 4096, 4, 4)
    held = [p] + digits_of(look_up(p, [word(BLK[c], 16) for c in range(16)]), 16, 4)
    third = look_up(p, [word(IDX[c], 8) + 4096 * word(HOLD[c][1:], 16) for c in range(16)])
    place = [jnp.int32(0)] + digits_of(third, 8, 4)
    holders = [p] + digits_of(third // 4096, 16, 4)
    lists = []
    for c in range(16):
        for core in range(2):
            flat = [slot for pair in PAIRS[c][core] for slot in pair]
            lists.append(len(PAIRS[c][core]) + 8 * word(flat + [0] * (8 - len(flat)), 8))
    todo = look_up(p * 2 + h, lists)
    pair_count = todo % 8
    todo = digits_of(todo // 8, 8, 8)

    needs = [[sum(1 << slot for slot in NEED[c][core]) for core in range(2)] for c in range(16)]
    need = digits_of(look_up(p * 2 + h, [needs[c][core] for c in range(16) for core in range(2)]), 2, SLOTS)
    sibling_need = digits_of(look_up(p * 2 + h, [needs[c][1 - core] for c in range(16) for core in range(2)]), 2, SLOTS)

    sibling = device(z, 1 - h, p)
    owner_grp = zl * 2 + zh
    mine = h == zh

    loads = []
    for k, rel in enumerate((0, 1, 3, 2)):
        loads.append(pltpu.make_async_copy(emb.at[group_of((z + rel) % 4)], stage.at[k], load_sem.at[k]))
        loads[-1].start()

    barrier = pltpu.get_barrier_semaphore()
    for rel in (1, 3):
        pl.semaphore_signal(barrier, inc=1, device_id=device((z + rel) % 4, h, p), device_id_type=MESH)
    for d in range(4):
        pl.semaphore_signal(barrier, inc=1, device_id=device(z, h, near[d]), device_id_type=MESH)
    pl.semaphore_signal(barrier, inc=1, device_id=sibling, device_id_type=MESH)
    from_z = 2 * h + zl
    for k in range(SLOTS):
        for core in range(2):
            def tell():
                pl.semaphore_signal(barrier, inc=1, device_id=device(from_z, core, holders[k]), device_id_type=MESH)
            if k == 0:
                pl.when(jnp.logical_not(jnp.logical_and(mine, h == core)))(tell)
            else:
                tell()

    def normalise(k):
        loads[k].wait()
        v = stage[k]
        total = jnp.sum(v * v, axis=-1, keepdims=True)
        return (v / jnp.sqrt(total + 1e-06)).astype(jnp.bfloat16)

    own_rows = pl.multiple_of(h * 128, 128)
    x[0, pl.ds(own_rows, 128), :] = normalise(0)
    pl.semaphore_wait(barrier, jnp.where(mine, 16, 17))

    def remote(src_ref, dst_ref, send_sem, recv_sem, to):
        return pltpu.make_async_remote_copy(
            src_ref=src_ref, dst_ref=dst_ref, send_sem=send_sem, recv_sem=recv_sem, device_id=to, device_id_type=MESH)

    def part_rows(t):
        return pl.ds(pl.multiple_of((t // 4) * 256 + h * 128 + (t % 4) * PIECE, PIECE), PIECE)

    def forward(d, t):
        rows = part_rows(t)
        return remote(x.at[src[d], rows, :], x.at[1 + (d ^ 1), rows, :], f_send.at[d, t], f_recv.at[d ^ 1, t],
                      device(z, h, near[d]))

    def arrival(s, t):
        rows = part_rows(t)
        return remote(x.at[s, rows, :], x.at[s, rows, :], f_send.at[s - 1, t], f_recv.at[s - 1, t],
                      device(z, h, near[s - 1]))

    def swap(k, half):
        rows = pl.ds(pl.multiple_of(k * 256 + h * 128 + half * 64, 64), 64)
        return remote(units.at[k - 1, pl.ds(half * 64, 64), :], x.at[0, rows, :], z_send.at[k - 1, half],
                      z_recv.at[k - 1, half], device((z + (1, 3, 2)[k - 1]) % 4, h, p))

    between = device((z + jnp.where(h == 0, 1, 3)) % 4, h, p)

    def relay_in(half):
        rows = pl.ds(half * 64, 64)
        return remote(units.at[2, rows, :], relay.at[rows, :], relay_send.at[0, half], relay_recv.at[half], between)

    def relay_out(half):
        rows = pl.ds(pl.multiple_of(3 * 256 + h * 128 + half * 64, 64), 64)
        return remote(relay.at[pl.ds(half * 64, 64), :], x.at[0, rows, :], relay_send.at[1, half], z_recv.at[2, half],
                      between)

    def share_rows(t, core):
        return pl.ds(pl.multiple_of((t // 2) * 256 + core * 128 + (t % 2) * 64, 64), 64)

    def share(s, t):
        rows = share_rows(t, h)
        return remote(x.at[s, rows, :], x.at[s, rows, :], c_send.at[s, t], c_recv.at[s, t], sibling)

    def shared(s, t):
        rows = share_rows(t, 1 - h)
        return remote(x.at[s, rows, :], x.at[s, rows, :], c_send.at[s, t], c_recv.at[s, t], sibling)

    def give(s, t):
        pl.when(sibling_need[s] == 1)(lambda: share(s, t).start())

    def send_own(t):
        for d in range(4):
            pl.when(src[d] == 0)(lambda d=d: forward(d, t).start())

    def send_held(t):
        for d in range(4):
            pl.when(src[d] != 0)(lambda d=d: forward(d, t).start())

    def receive(links, t):
        for s in range(1, SLOTS):
            pl.when(dep[s - 1] == links)(lambda s=s: arrival(s, t).wait_recv())

    def give_held(links, t):
        for s in range(1, SLOTS):
            pl.when(dep[s - 1] == links)(lambda s=s: give(s, t // 2))

    for t in range(4):
        send_own(t)
    units[0] = normalise(1)
    for half in range(2):
        swap(1, half).start()
    units[1] = normalise(2)
    for half in range(2):
        swap(2, half).start()
    units[2] = normalise(3)
    for half in range(2):
        relay_in(half).start()
    ids_copy = remote(ids_in, ids_got, id_send, id_recv, sibling)
    ids_copy.start()
    give(0, 0)
    give(0, 1)
    row_best[...] = jnp.full_like(row_best, -1.0)
    col_best[...] = jnp.full_like(col_best, -1.0)
    row_line[...] = jnp.full_like(row_line, -1.0)

    ids_copy.wait_recv()
    ids_cols[...] = jnp.zeros_like(ids_cols)
    for s in range(SLOTS):
        for t in range(4):
            for core in range(2):
                unit = held[s] * 8 + 2 * ((z + REL[t]) % 4) + core
                got = jnp.where(mine, ids_in[pl.ds(unit, 1), :], ids_got[pl.ds(unit, 1), :])
                ids_cols[pl.ds(s * 8 + 2 * t + core, 1), :] = got.astype(jnp.float32)
    turned = ids_cols[...].T
    for j in range(SLOTS * 8):
        ids_rows[j] = jnp.broadcast_to(turned[:, j:j + 1], (128, 128))

    def strip(a, t, b, count, diagonal=False):
        sim = lax.dot_general(x[a, 256 * t:256 * t + 256, :], x[b, 0:256 * count, :], (((1,), (1,)), ((), ())),
                              preferred_element_type=jnp.float32)
        for r in range(4):
            unit, first_row = a * 8 + 2 * t + r // 2, 64 * (r % 2)
            row_ids = ids_rows[unit, first_row:first_row + 64]
            best = row_best[unit, first_row:first_row + 64]
            for c in range(2 * count):
                keep = row_ids == ids_cols[pl.ds(b * 8 + c, 1), :]
                if diagonal and c // 2 == t:
                    row = lax.broadcasted_iota(jnp.int32, (64, 128), 0) + 64 * r
                    col = lax.broadcasted_iota(jnp.int32, (64, 128), 1) + 128 * (c % 2)
                    keep = jnp.logical_and(keep, row != col)
                kept = jnp.where(keep, sim[64 * r:64 * r + 64, 128 * c:128 * c + 128], jnp.float32(-1.0))
                down = jnp.max(kept.reshape(8, 8, 128), axis=0)
                col_best[b * 8 + c] = jnp.maximum(col_best[b * 8 + c], down)
                best = jnp.maximum(best, kept)
            row_best[unit, first_row:first_row + 64] = best

    def compare(t, j):
        a, b = todo[0], todo[1]
        for k in range(1, 4):
            a = jnp.where(j == k, todo[2 * k], a)
            b = jnp.where(j == k, todo[2 * k + 1], b)
        strip(a, t, b, t + 1)
        if t:
            strip(b, t, a, t)

    def finish_rows(t):
        pl.when(h == 1)(lambda: strip(0, t, 0, t + 1, diagonal=True))
        for s in range(SLOTS):
            @pl.when(need[s] == 1)
            def _():
                for core in range(2):
                    unit = s * 8 + 2 * t + core
                    row_line[unit:unit + 1, :] = jnp.max(row_best[unit].T, axis=0, keepdims=True)

    def wait_shared(m):
        for s in range(SLOTS):
            @pl.when(need[s] == 1)
            def _():
                for half in range(2):
                    shared(s, 2 * m + half).wait_recv()

    def own_half_ready(m, half):
        send_own(4 * m + 2 * half)
        send_own(4 * m + 2 * half + 1)
        give(0, 2 * m + half)

    def own_block(k):
        @pl.when(k == 2)
        def _():
            swap(1, 0).wait_recv()
            own_half_ready(1, 0)

        @pl.when(k == 4)
        def _():
            swap(1, 1).wait_recv()
            own_half_ready(1, 1)
            swap(2, 0).wait_recv()
            own_half_ready(2, 0)

        @pl.when(k == 6)
        def _():
            relay_in(0).wait_recv()
            relay_out(0).start()

        @pl.when(k == 7)
        def _():
            relay_in(1).wait_recv()
            relay_out(1).start()

        @pl.when(k == 8)
        def _():
            swap(2, 1).wait_recv()
            own_half_ready(2, 1)

        @pl.when(k == 10)
        def _():
            relay_out(0).wait_recv()
            own_half_ready(3, 0)

        @pl.when(k == 11)
        def _():
            relay_out(1).wait_recv()
            own_half_ready(3, 1)

    def pass_on(k):
        receive(1, k - 1)
        send_held(k - 1)
        pl.when(k % 2 == 0)(lambda: give_held(1, k - 1))

    def take(t):
        receive(2, t)
        pl.when(t % 2 == 1)(lambda: give_held(2, t))

    @pl.loop(1, 9)
    def _(k):
        pass_on(k)
        own_block(k)
        pl.when(k >= 4)(lambda: take(k - 4))

    for m in range(2):
        @pl.loop(9 + 4 * m, 13 + 4 * m)
        def _(k):
            j = k - 9 - 4 * m
            pass_on(k)
            if m == 0:
                own_block(k)
            pl.when(j == 0)(lambda: wait_shared(m))
            pl.when(j < pair_count)(lambda: compare(m, j))
            take(k - 4)
        finish_rows(m)

    wait_shared(2)

    @pl.loop(0, 4)
    def _(j):
        pl.when(j < pair_count)(lambda: compare(2, j))
        pl.when(j < 3)(lambda: take(13 + j))
    finish_rows(2)
    wait_shared(3)

    @pl.loop(0, pair_count)
    def _(j):
        compare(3, j)
    finish_rows(3)

    for s in range(SLOTS):
        for t in range(4):
            z_of = (z + REL[t]) % 4
            for core in range(2):
                j = s * 8 + 2 * t + core
                both = jnp.maximum(row_line[j:j + 1, :], jnp.max(col_best[j], axis=0, keepdims=True))
                part[s * 2 + z_of // 2, pl.ds(2 * (z_of % 2) + core, 1), :] = both
        for half in range(2):
            copy = remote(part.at[s * 2 + half], parts_got.at[place[s] * 2 + h], r_send.at[s * 2 + half],
                          r_recv.at[place[s] * 2 + h], (owner_grp, held[s] * 2 + half))
            if s == 0:
                keep_it = jnp.logical_and(mine, zh == half)
                pl.when(jnp.logical_not(keep_it))(copy.start)

                @pl.when(keep_it)
                def _():
                    parts_got[h] = part[half]
            else:
                copy.start()

    ids_copy.wait_send()
    for half in range(2):
        for copy in (swap(1, half), swap(2, half), relay_in(half), relay_out(half)):
            copy.wait_send()
    for d in range(4):
        for t in range(STEPS):
            forward(d, t).wait_send()
    for s in range(SLOTS):
        for t in range(8):
            pl.when(sibling_need[s] == 1)(lambda s=s, t=t: share(s, t).wait_send())
    best = None
    for k in range(2 * SLOTS):
        got = remote(parts_got.at[k], parts_got.at[k], r_send.at[k], r_recv.at[k], sibling)
        if k < 2:
            pl.when(jnp.logical_not(jnp.logical_and(mine, h == k)))(got.wait_recv)
        else:
            got.wait_recv()
        best = parts_got[k] if best is None else jnp.maximum(best, parts_got[k])
    out[...] = best

    for s in range(SLOTS):
        for half in range(2):
            copy = remote(part.at[s * 2 + half], parts_got.at[place[s] * 2 + h], r_send.at[s * 2 + half],
                          r_recv.at[place[s] * 2 + h], (owner_grp, held[s] * 2 + half))
            if s == 0:
                pl.when(jnp.logical_not(jnp.logical_and(mine, zh == half)))(copy.wait_send)
            else:
                copy.wait_send()


def on_device(embeddings, cluster_ids):
    emb = embeddings.reshape(4, 128, D)
    ids = cluster_ids.reshape(128, 128)
    dma = pltpu.SemaphoreType.DMA
    best = pl.pallas_call(
        kernel,
        out_shape=jax.ShapeDtypeStruct((4, 128), jnp.float32),
        in_specs=[pl.BlockSpec(memory_space=pl.ANY), pl.BlockSpec(memory_space=pltpu.VMEM)],
        out_specs=pl.BlockSpec(memory_space=pltpu.VMEM),
        scratch_shapes=[
            pltpu.VMEM((SLOTS, 1024, D), jnp.bfloat16),
            pltpu.VMEM((3, 128, D), jnp.bfloat16),
            pltpu.VMEM((4, 128, D), jnp.float32),
            pltpu.VMEM((128, 128), jnp.int32),
            pltpu.VMEM((SLOTS * 8, 128, 128), jnp.float32),
            pltpu.VMEM((128, 128), jnp.float32),
            pltpu.VMEM((SLOTS * 8, 128, 128), jnp.float32),
            pltpu.VMEM((SLOTS * 8, 8, 128), jnp.float32),
            pltpu.VMEM((SLOTS * 8, 128), jnp.float32),
            pltpu.VMEM((2 * SLOTS, 4, 128), jnp.float32),
            pltpu.VMEM((2 * SLOTS, 4, 128), jnp.float32),
            pltpu.VMEM((128, D), jnp.bfloat16),
            dma((4,)), dma, dma, dma((3, 2)), dma((3, 2)), dma((2, 2)), dma((2,)), dma((4, STEPS)), dma((4, STEPS)),
            dma((SLOTS, 8)), dma((SLOTS, 8)), dma((2 * SLOTS,)), dma((2 * SLOTS,)),
        ],
        compiler_params=pltpu.CompilerParams(
            collective_id=0, has_side_effects=True, vmem_limit_bytes=60 * 1024 * 1024),
        cost_estimate=pl.CostEstimate(flops=7 * 10**9, bytes_accessed=2 * 10**6, transcendentals=0),
        name="best_match",
    )(emb, ids)
    return best.reshape(1, 512)


def solution(mesh):
    placed = (P(None, "grp", "blk", None, None), P("grp", None))
    return jax.shard_map(
        on_device, mesh=mesh, in_specs=placed, out_specs=P("grp", "blk"), check_vma=False
    )
```

profile of v0, /device:TPU:1, one launch (start us, length us, event | category | flops | bytes accessed | tf_op | source)
XLA Modules:
  0.0 47.4 jit_solution(17871586780860858001)
XLA Ops:
  0.0 46.1 %best_match.1 = f32[4,128]{1,0:T(4,128)} custom-call(f32[4,128,768]{2,1,0:T(8,128)} %bitcast.4, s32[128,128]{1,0:T(8,128)} %bitcast.5), custom_call_target="tpu_custom_call" | custom-call | flops 7000000000 | bytes 2000000 | tf_op jit(solution)/shard_map/best_match/pallas_call | solution.py:415
  46.1 1.3 %copy.4 = f32[1,512]{1,0:T(1,128)} copy(f32[1,512]{1,0:T(1,128)} %bitcast.3) | data formatting | bytes 4096
where the time goes:
time: 47.6 us; the launch traced here: 47.4 us
  Pallas kernels  46.1 us (97%)
  local copies, waits for them, and re-layouts  1.26 us (3%)
    pallas_call x1, Pallas kernels, on_device(): pl.pallas_call(kernel, out_shape=jax.ShapeDtypeStruct((4, 128), jnp.float...  46.1 us
    unnamed x1, local copies, waits for them, and re-layouts  1.26 us

commit v1 on v0

--- a/solution.py
+++ b/solution.py
@@ -231,23 +231,26 @@
         ids_rows[j] = jnp.broadcast_to(turned[:, j:j + 1], (128, 128))
 
     def strip(a, t, b, count, diagonal=False):
-        sim = lax.dot_general(x[a, 256 * t:256 * t + 256, :], x[b, 0:256 * count, :], (((1,), (1,)), ((), ())),
+        sim = lax.dot_general(x[b, 0:256 * count, :], x[a, 256 * t:256 * t + 256, :], (((1,), (1,)), ((), ())),
                               preferred_element_type=jnp.float32)
-        for r in range(4):
-            unit, first_row = a * 8 + 2 * t + r // 2, 64 * (r % 2)
+        col_ids = [ids_cols[pl.ds(a * 8 + 2 * t + c, 1), :] for c in range(2)]
+        downs = [col_best[a * 8 + 2 * t + c] for c in range(2)]
+        for r in range(4 * count):
+            unit, first_row = b * 8 + r // 2, 64 * (r % 2)
             row_ids = ids_rows[unit, first_row:first_row + 64]
             best = row_best[unit, first_row:first_row + 64]
-            for c in range(2 * count):
-                keep = row_ids == ids_cols[pl.ds(b * 8 + c, 1), :]
-                if diagonal and c // 2 == t:
-                    row = lax.broadcasted_iota(jnp.int32, (64, 128), 0) + 64 * r
-                    col = lax.broadcasted_iota(jnp.int32, (64, 128), 1) + 128 * (c % 2)
+            for c in range(2):
+                keep = row_ids == col_ids[c]
+                if diagonal and r // 4 == t:
+                    row = lax.broadcasted_iota(jnp.int32, (64, 128), 0) + 64 * (r % 4)
+                    col = lax.broadcasted_iota(jnp.int32, (64, 128), 1) + 128 * c
                     keep = jnp.logical_and(keep, row != col)
                 kept = jnp.where(keep, sim[64 * r:64 * r + 64, 128 * c:128 * c + 128], jnp.float32(-1.0))
-                down = jnp.max(kept.reshape(8, 8, 128), axis=0)
-                col_best[b * 8 + c] = jnp.maximum(col_best[b * 8 + c], down)
+                downs[c] = jnp.maximum(downs[c], jnp.max(kept.reshape(8, 8, 128), axis=0))
                 best = jnp.maximum(best, kept)
             row_best[unit, first_row:first_row + 64] = best
+        for c in range(2):
+            col_best[a * 8 + 2 * t + c] = downs[c]
 
     def compare(t, j):
         a, b = todo[0], todo[1]
@@ -258,14 +261,8 @@
         if t:
             strip(b, t, a, t)
 
-    def finish_rows(t):
+    def own_pair(t):
         pl.when(h == 1)(lambda: strip(0, t, 0, t + 1, diagonal=True))
-        for s in range(SLOTS):
-            @pl.when(need[s] == 1)
-            def _():
-                for core in range(2):
-                    unit = s * 8 + 2 * t + core
-                    row_line[unit:unit + 1, :] = jnp.max(row_best[unit].T, axis=0, keepdims=True)
 
     def wait_shared(m):
         for s in range(SLOTS):
@@ -342,7 +339,7 @@
             pl.when(j == 0)(lambda: wait_shared(m))
             pl.when(j < pair_count)(lambda: compare(m, j))
             take(k - 4)
-        finish_rows(m)
+        own_pair(m)
 
     wait_shared(2)
 
@@ -350,13 +347,19 @@
     def _(j):
         pl.when(j < pair_count)(lambda: compare(2, j))
         pl.when(j < 3)(lambda: take(13 + j))
-    finish_rows(2)
+    own_pair(2)
     wait_shared(3)
 
     @pl.loop(0, pair_count)
     def _(j):
         compare(3, j)
-    finish_rows(3)
+    own_pair(3)
+
+    for s in range(SLOTS):
+        @pl.when(need[s] == 1)
+        def _():
+            for unit in range(s * 8, s * 8 + 8):
+                row_line[unit:unit + 1, :] = jnp.max(row_best[unit].T, axis=0, keepdims=True)
 
     for s in range(SLOTS):
         for t in range(4):

time: 47.6 us -> 47.8 us (level)
  no operation moved by 1% of the time
where the time goes in v1:
time: 47.8 us; the launch traced here: 47.6 us
  Pallas kernels  46.3 us (97%)
  local copies, waits for them, and re-layouts  1.26 us (3%)
    pallas_call x1, Pallas kernels, on_device(): pl.pallas_call(kernel, out_shape=jax.ShapeDtypeStruct((4, 128), jnp.float...  46.3 us
    unnamed x1, local copies, waits for them, and re-layouts  1.26 us

profile of v1, /device:TPU:1, one launch (start us, length us, event | category | flops | bytes accessed | tf_op | source)
XLA Modules:
  0.0 47.6 jit_solution(466333760248405646)
XLA Ops:
  0.0 46.3 %best_match.1 = f32[4,128]{1,0:T(4,128)} custom-call(f32[4,128,768]{2,1,0:T(8,128)} %bitcast.4, s32[128,128]{1,0:T(8,128)} %bitcast.5), custom_call_target="tpu_custom_call" | custom-call | flops 7000000000 | bytes 2000000 | tf_op jit(solution)/shard_map/best_match/pallas_call | solution.py:418
  46.3 1.3 %copy.4 = f32[1,512]{1,0:T(1,128)} copy(f32[1,512]{1,0:T(1,128)} %bitcast.3) | data formatting | bytes 4096
